TPU v7x, 32 devices: a whole 2x2x4 slice. The times are simulated.
32 devices in a mesh: section: 2 (over x), dp: 16 (over z, y, core).
Axes of the slice: x: 2, y: 2, z: 4, core: 2. Of those that a mesh axis runs over, the one named last changes fastest.
Arguments:
- visible_tokens: float32 [32, 256, 768], P('dp'), may hold values from -100 to 100
- cotangent: float32 [32, 1024, 512], P('dp'), may hold values from -6 to 6
- chip_sizes: int32 [32, 4], P('dp'), may hold values from 0 to 1024, as said below
- ground_distance: int32 [32, 4], P('dp'), may hold values from 1 to 32
- visible_slots: int32 [32, 256], P('dp'), may hold values from -1 to 1023, as said below
- encoder_gains: float32 [2, 768], replicated, may hold values from 0.5 to 1.5
- encoder_shifts: float32 [2, 768], replicated, may hold values from -4 to 4
- encoder_biases: float32 [2, 768], replicated, may hold values from -4 to 4
- encoder_attend: bfloat16 [768, 2304], replicated, may hold values from -0.21875 to 0.21875
- encoder_merge: bfloat16 [768, 768], replicated, may hold values from -1.75 to 1.75
- encoder_expand: bfloat16 [768, 3072], replicated, may hold values from -0.21875 to 0.21875
- encoder_inner: float32 [3072], replicated, may hold values from -4 to 4
- encoder_shrink: bfloat16 [3072, 768], replicated, may hold values from -0.109375 to 0.109375
- decoder_entry: bfloat16 [768, 512], replicated, may hold values from -0.21875 to 0.21875
- decoder_biases: float32 [3, 512], replicated, may hold values from -4 to 4
- mask_token: float32 [512], replicated, may hold values from -5 to 5
- decoder_gains: float32 [2, 512], replicated, may hold values from 0.5 to 1.5
- decoder_shifts: float32 [2, 512], replicated, may hold values from -4 to 4
- decoder_attend: bfloat16 [512, 768], replicated, may hold values from -0.25 to 0.25
- decoder_merge: bfloat16 [256, 512], replicated, may hold values from -4 to 4
- decoder_widen_weight: bfloat16 [512, 2048], replicated, may hold values from -0.25 to 0.25
- decoder_inner: float32 [2048], replicated, may hold values from -4 to 4
- decoder_shrink: bfloat16 [2048, 512], replicated, may hold values from -0.125 to 0.125
Outputs:
- boundary_grads: float32 [2, 32, 256, 768], P('section', 'dp')
- statistics: float32 [8], replicated
- encoder_gains_grad: float32 [2, 768], P(None, ('section', 'dp'))
- encoder_shifts_grad: float32 [2, 768], P(None, ('section', 'dp'))
- encoder_biases_grad: float32 [2, 768], P(None, ('section', 'dp'))
- encoder_attend_grad: float32 [768, 2304], P(('section', 'dp'))
- encoder_merge_grad: float32 [768, 768], P(None, ('section', 'dp'))
- encoder_expand_grad: float32 [768, 3072], P(('section', 'dp'))
- encoder_inner_grad: float32 [3072], P(('section', 'dp'))
- encoder_shrink_grad: float32 [3072, 768], P(('section', 'dp'))
- decoder_entry_grad: float32 [768, 512], P(('section', 'dp'))
- decoder_biases_grad: float32 [3, 512], P(None, ('section', 'dp'))
- mask_token_grad: float32 [512], P(('section', 'dp'))
- decoder_gains_grad: float32 [2, 512], P(None, ('section', 'dp'))
- decoder_shifts_grad: float32 [2, 512], P(None, ('section', 'dp'))
- decoder_attend_grad: float32 [512, 768], P(('section', 'dp'))
- decoder_merge_grad: float32 [256, 512], P(None, ('section', 'dp'))
- decoder_expand_grad: float32 [512, 2048], P(('section', 'dp'))
- decoder_inner_grad: float32 [2048], P(('section', 'dp'))
- decoder_shrink_grad: float32 [2048, 512], P(('section', 'dp'))
Inputs may be any that keep to these rules, and one draw needn't show every extreme that they name: `chip_sizes`: each pack's slots hold, in order, either one chip of 1024 patches or two to 4 chips of 256 patches, then zeros. The first pack holds one chip of 1024, the second 4 chips of 256. `visible_slots`: encoder slots follow the pack's chips in order: a chip of n patches owns n / 4 consecutive slots, each naming a different decoder slot of that chip; the slots after the last chip hold -1.
All inputs are finite; a program needn't handle non-finite values.
Results may differ from a plain program's by a relative error of at most 0.017.
Values may be sent and summed in bfloat16 or wider, within the bound.
A program may use at most 320 MiB of HBM per device.

v0:
```python
import functools
import types

import jax
import jax.numpy as jnp
import numpy as np
from jax import lax
from jax.experimental import pallas as pl
from jax.experimental.pallas import tpu as pltpu
from jax.sharding import PartitionSpec as P

DE = 768
DD = 512
TILE = 256
BLOCK = 512
NEGATIVE = -1e30
F32, BF16 = jnp.float32, jnp.bfloat16
MESH_ID = pl.DeviceIdType.MESH

CANON = ("x", "z2", "z1", "y")
ROUTES = (("x", "y", "z1", "z2"), ("y", "x", "z1", "z2"), ("z1", "z2", "x", "y"))
UNIT = 1536
LAG = 2
DECODER_PLAN = types.SimpleNamespace(widths=(2, 2, 1), chunks=7, slots=7, ring=3, span=640)
ENCODER_PLAN = types.SimpleNamespace(widths=(3, 6, 3), chunks=9, slots=3, ring=3, span=1536)
TAIL_PLAN = types.SimpleNamespace(widths=(2, 3, 1), chunks=2, slots=2, ring=2, span=768)

DECODER_EXPAND, DECODER_SHRINK, DECODER_MERGE = (0, 16, 2048), (2048, 64, 512), (4096, 16, 256)
ENTRY, DECODER_ATTEND = (0, 24, 512), (768, 16, 768)
ENCODER_SHRINK = tuple((UNIT * (1 + part), 96, 256) for part in range(3))
ENCODER_EXPAND = tuple((UNIT * (4 + part), 24, 1024) for part in range(3))
ENCODER_ATTEND = ((UNIT * 7, 24, 1024), (UNIT * 8, 24, 1024), (0, 24, 256))
ENCODER_MERGE = (384, 24, 768)


def dot(a, b):
    return jnp.dot(a, b, preferred_element_type=F32)


def dot_nt(a, b):
    return lax.dot_general(a, b, (((1,), (1,)), ((), ())), preferred_element_type=F32)


def dot_tn(a, b):
    return lax.dot_general(a, b, (((0,), (0,)), ((), ())), preferred_element_type=F32)


def low(value):
    return value.astype(BF16)


def standardize(values):
    centered = values - jnp.mean(values, axis=-1, keepdims=True)
    inverse = lax.rsqrt(jnp.mean(centered * centered, axis=-1, keepdims=True) + 1e-05)
    return centered * inverse, inverse


def norm_back(unit, inverse, gain, grad):
    inner = grad * gain
    return inverse * (
        inner
        - jnp.mean(inner, axis=-1, keepdims=True)
        - unit * jnp.mean(inner * unit, axis=-1, keepdims=True)
    )


def row_sum(values):
    return jnp.sum(values, axis=0, keepdims=True)


def gelu_pair(before):
    half = 0.5 * (1.0 + lax.erf(before * 0.7071067811865476))
    density = jnp.exp(-0.5 * before * before) * 0.3989422804014327
    return before * half, half + before * density


def chip_of(places, sizes, pack):
    end = sizes[pack, 0]
    chip = (places >= end).astype(jnp.int32)
    for slot in range(1, 4):
        end = end + sizes[pack, slot]
        chip = chip + (places >= end).astype(jnp.int32)
    return chip


def iota(shape, dimension):
    return lax.broadcasted_iota(jnp.int32, shape, dimension)


def aligned(start, size, unit):
    if isinstance(start, int):
        return slice(start, start + size)
    return pl.ds(pl.multiple_of(start, unit), size)


def pair_lanes(pair, base=0):
    return aligned(base + pair * 128, 128, 128)


def head_rows(pair, half, base=0):
    return aligned(base + pair * 128 + half * 64, 64, 64)


def rows_of(tile, size=TILE):
    return aligned(tile * size, size, size)


def only(values, half):
    return jnp.where(iota((1, 128), 1) // 64 == half, values, jnp.zeros_like(values))


def fetch(pairs, sems):
    copies = [
        pltpu.make_async_copy(source, target, sems.at[i]) for i, (source, target) in enumerate(pairs)
    ]
    for copy in copies:
        copy.start()
    return copies


def store_packed(put, first, place, value):
    offset, count, width = place
    value = value.reshape(-1, count, width)
    shards = slice(first, first + value.shape[0]) if isinstance(first, int) else pl.ds(first, value.shape[0])
    for piece in range(count // 16):
        put(shards, offset + piece * width, value[:, piece * 16 : piece * 16 + 16])
    if count % 16:
        half = width // 2
        rest = value[:, count - 8 :]
        rest = jnp.concatenate([rest[:, :, :half], rest[:, :, half:]], axis=1)
        put(shards, offset + count // 16 * width, rest)


def halves(shards, value):
    pairs = value.reshape(value.shape[0] // 2, 2, *value.shape[1:])
    if isinstance(shards, slice):
        return slice(shards.start // 2, shards.stop // 2), pairs[:, 0], pairs[:, 1]
    return pl.ds(shards.start // 2, shards.size // 2), pairs[:, 0], pairs[:, 1]


def place_of(names, bits):
    index = 0
    for name in names:
        index = index * 2 + bits[name]
    return index


def left_after(route, stage):
    return tuple(name for name in CANON if name not in route[:stage])


def choices(names):
    for number in range(2 ** len(names)):
        yield {name: (number >> (len(names) - 1 - i)) & 1 for i, name in enumerate(names)}


def neighbours():
    section = lax.axis_index("section")
    data = lax.axis_index("dp")
    mine = {"x": section, "c": data % 2, "y": data // 2 % 2, "z1": data // 4 % 2, "z2": data // 8 % 2}
    partner = {"x": (1 - section, data)}
    for name, step in {"c": 1, "y": 2, "z1": 4, "z2": 8}.items():
        partner[name] = (section, data + step * (1 - 2 * mine[name]))
    return mine, partner


def greet(partner):
    barrier = pltpu.get_barrier_semaphore()
    for name in ("c",) + CANON:
        pl.semaphore_signal(barrier, inc=1, device_id=partner[name], device_id_type=MESH_ID)


def await_greetings():
    pl.semaphore_wait(pltpu.get_barrier_semaphore(), 5)


def remote(source, target, send, recv, device):
    return pltpu.make_async_remote_copy(
        src_ref=source,
        dst_ref=target,
        send_sem=send,
        recv_sem=recv,
        device_id=device,
        device_id_type=MESH_ID,
    )


def reducer(plan, mine, partner, out, refs):
    chunks, slots, span, ring = plan.chunks, plan.slots, plan.span, plan.ring
    progress = types.SimpleNamespace(sent=0)
    own, staging, first = refs[:3]
    sent, got = refs[3:15], refs[15:27]
    first_send, first_recv, send_sem, recv_sem = refs[27:31]

    def first_copy(chunk):
        return remote(staging.at[chunk % slots], first.at[chunk], first_send.at[chunk], first_recv.at[chunk], partner["c"])

    def stage_copy(route, stage, chunk):
        return remote(
            sent[route * 4 + stage].at[chunk % ring],
            got[route * 4 + stage].at[chunk],
            send_sem.at[route, stage, chunk],
            recv_sem.at[route, stage, chunk],
            partner[ROUTES[route][stage]],
        )

    def total(route, stage, chunk, bits):
        spot = place_of(CANON, bits)
        cols = slice(sum(plan.widths[:route]) * 128, sum(plan.widths[: route + 1]) * 128)
        value = own[chunk, spot, :, cols].astype(F32) + first[chunk, spot, :, cols].astype(F32)
        for earlier in range(stage):
            names = left_after(ROUTES[route], earlier + 1)
            value = value + got[route * 4 + earlier][chunk, place_of(names, bits)].astype(F32)
        return value

    def advance(stage, chunk):
        for route in range(3):
            if stage:
                stage_copy(route, stage - 1, chunk).wait_recv()
            else:
                first_copy(chunk).wait_recv() if route == 0 else None
            if stage < 4:

                @pl.when(chunk >= ring)
                def _(route=route):
                    stage_copy(route, stage, chunk - ring).wait_send()

        values = []
        for route in range(3):
            path = ROUTES[route]
            if stage == 4:
                values.append(total(route, 4, chunk, mine))
                continue
            names = left_after(path, stage + 1)
            for free in choices(names):
                bits = dict(mine)
                bits[path[stage]] = 1 - mine[path[stage]]
                bits.update(free)
                values.append((route, place_of(names, free), low(total(route, stage, chunk, bits))))
        if stage == 4:
            out[chunk] = jnp.concatenate(values, axis=1)
            return
        for route, spot, value in values:
            sent[route * 4 + stage][chunk % ring, spot] = value
        for route in range(3):
            stage_copy(route, stage, chunk).start()

    def turn(number):
        for stage in range(4, -1, -1):
            chunk = number - LAG * stage
            pl.when((chunk >= 0) & (chunk < chunks))(functools.partial(advance, stage, chunk))

    def put(shards, column, value):
        shards, even, odd = halves(shards, value)
        kept = low(jnp.where(mine["c"] == 0, even, odd))
        given = low(jnp.where(mine["c"] == 0, odd, even))
        width = value.shape[2]
        done = 0
        while done < width:
            chunk, start = divmod(column + done, span)
            size = min(width - done, span - start)
            own[chunk, shards, :, start : start + size] = kept[:, :, done : done + size]
            staging[chunk % slots, shards, :, start : start + size] = given[:, :, done : done + size]
            done += size

    def put_unit(unit):
        def put(shards, column, value):
            shards, even, odd = halves(shards, value)
            cols = slice(column, column + value.shape[2])
            own[unit, shards, :, cols] = low(jnp.where(mine["c"] == 0, even, odd))
            staging[unit % slots, shards, :, cols] = low(jnp.where(mine["c"] == 0, odd, even))

        @pl.when(unit >= slots)
        def _():
            first_copy(unit - slots).wait_send()

        return put

    def send(column):
        while (progress.sent + 1) * span <= column:
            first_copy(progress.sent).start()
            progress.sent += 1

    def close():
        for chunk in range(max(0, chunks - slots), chunks):
            first_copy(chunk).wait_send()
        for chunk in range(chunks - ring, chunks):
            for route in range(3):
                for stage in range(4):
                    stage_copy(route, stage, chunk).wait_send()

    return types.SimpleNamespace(
        own=own, staging=staging, turn=turn, put=put, put_unit=put_unit, first_copy=first_copy, send=send, close=close
    )


def reducer_scratch(plan):
    stages = [(width, block) for width in plan.widths for block in (8, 4, 2, 1)]
    return (
        [
            pltpu.VMEM((plan.chunks, 16, 16, plan.span), BF16),
            pltpu.VMEM((plan.slots, 16, 16, plan.span), BF16),
            pltpu.VMEM((plan.chunks, 16, 16, plan.span), BF16),
        ]
        + [pltpu.VMEM((plan.ring, block, 16, width * 128), BF16) for width, block in stages]
        + [pltpu.VMEM((plan.chunks, block, 16, width * 128), BF16) for width, block in stages]
        + [
            pltpu.SemaphoreType.DMA((plan.chunks,)),
            pltpu.SemaphoreType.DMA((plan.chunks,)),
            pltpu.SemaphoreType.DMA((3, 4, plan.chunks)),
            pltpu.SemaphoreType.DMA((3, 4, plan.chunks)),
        ]
    )


def put_into(parts):
    span = parts.shape[-1]

    def put(shards, column, value):
        shards, *pair = halves(shards, value)
        width = value.shape[2]
        done = 0
        while done < width:
            chunk, start = divmod(column + done, span)
            size = min(width - done, span - start)
            for core in range(2):
                parts[chunk, core, shards, :, start : start + size] = low(pair[core][:, :, done : done + size])
            done += size

    return put


def put_unit_into(parts, unit):
    def put(shards, column, value):
        shards, *pair = halves(shards, value)
        for core in range(2):
            parts[unit, core, shards, :, column : column + value.shape[2]] = low(pair[core])

    return put


def vmem_spec():
    return pl.BlockSpec(memory_space=pltpu.VMEM)


def any_spec():
    return pl.BlockSpec(memory_space=pl.ANY)


def smem_spec():
    return pl.BlockSpec(memory_space=pltpu.SMEM)


def encoder_forward_kernel(
    sizes, gains, shifts, biases, inner, tokens, attend_far, merging_far, expand_far, shrink_far,
    sent, vectors, *refs,
):
    far = refs[:9]
    normed, mixed, turned, probs, context, middle, normed_two, active, slope = refs[9:18]
    hidden, attend, merging, expand, shrink, context_turned, load_sem, save_sem = refs[18:]
    pack = lax.axis_index("section")
    loads = fetch(
        [
            (tokens.at[pack], hidden),
            *[(attend_far.at[:, i * 768 : i * 768 + 768], attend.at[:, i * 768 : i * 768 + 768]) for i in range(3)],
            (merging_far, merging),
            *[(expand_far.at[:, i * 1024 : i * 1024 + 1024], expand.at[:, i * 1024 : i * 1024 + 1024]) for i in range(3)],
            *[(shrink_far.at[i * 1024 : i * 1024 + 1024], shrink.at[i * 1024 : i * 1024 + 1024]) for i in range(3)],
        ],
        load_sem,
    )
    saves = []

    def save(*numbers):
        for number in numbers:
            copy = pltpu.make_async_copy(refs[9 + number], far[number], save_sem.at[number])
            copy.start()
            saves.append(copy)

    vectors[...] = jnp.zeros_like(vectors)
    key_chip = chip_of(4 * iota((TILE, 1), 0), sizes, pack)
    own_chip = chip_of(4 * iota((1, TILE), 1), sizes, pack)
    valid = (key_chip < 4).astype(F32)
    loads[0].wait()
    values = hidden[...]
    vectors[10:11, :768] = row_sum(valid * values * values)
    unit, _ = standardize(values)
    norm = low(unit * gains[0:1] + shifts[0:1])
    normed[...] = norm
    for part in range(3):
        cols = slice(part * 768, part * 768 + 768)
        loads[1 + part].wait()
        mix = dot(norm, attend[:, cols])
        mixed[:, cols] = low(mix)
        if part:
            turned[(part - 1) * 768 : part * 768] = low(mix.T)
    save(0, 1, 2)

    def score(head):
        pair, half = divmod(head, 2)
        query = only(mixed[:, pair_lanes(pair)], half) * BF16(0.125)
        return dot_nt(mixed[:, pair_lanes(pair, 768)], query)

    ready = [score(0), score(1)]
    for head in range(12):
        if head + 2 < 12:
            ready.append(score(head + 2))
        scores = jnp.where(key_chip == own_chip, ready[head], NEGATIVE)
        expos = jnp.exp(scores - jnp.max(scores, axis=0, keepdims=True))
        prob = low(expos * (1.0 / jnp.sum(expos, axis=0, keepdims=True)))
        probs[head] = prob
        context_turned[head * 64 : head * 64 + 64] = dot(turned[768 + head * 64 : 832 + head * 64], prob)

    mingled = low(context_turned[...].T)
    context[...] = mingled
    save(3, 4)
    loads[4].wait()
    attention = dot(mingled, merging[...]) + biases[0:1]
    vectors[11:12, :768] = row_sum(valid * attention * attention)
    center = hidden[...] + attention
    middle[...] = center
    unit, _ = standardize(center)
    norm = low(unit * gains[1:2] + shifts[1:2])
    normed_two[...] = norm
    save(5, 6)
    feed = jnp.zeros_like(center)
    def widened(part):
        if part % 2 == 0:
            loads[5 + part // 2].wait()
        cols = slice(part * 512, part * 512 + 512)
        return dot(norm, expand[:, cols]) + inner[:, cols]

    ready = [widened(0)]
    for part in range(6):
        if part < 5:
            ready.append(widened(part + 1))
        cols = slice(part * 512, part * 512 + 512)
        value, slant = gelu_pair(ready[part])
        value = low(value)
        active[:, cols] = value
        slope[part // 2, :, part % 2 * 512 : part % 2 * 512 + 512] = slant
        if part % 2 == 0:
            loads[8 + part // 2].wait()
        feed = feed + dot(value, shrink[cols])
    save(7, 8)
    feed = feed + biases[1:2]
    vectors[12:13, :768] = row_sum(valid * feed * feed)
    output = center + feed
    vectors[13:14, :768] = row_sum(valid * output * output)
    vectors[14:15, :768] = jnp.broadcast_to(row_sum(valid), (1, 768))
    sent[...] = low(output)
    for copy in saves:
        copy.wait()


def encoder_forward_call(sizes, tokens, gains, shifts, biases, attend, merging, expand, inner, shrink):
    shapes = (
        ((256, 768), BF16),
        ((256, 2304), BF16),
        ((1536, 256), BF16),
        ((12, 256, 256), BF16),
        ((256, 768), BF16),
        ((256, 768), F32),
        ((256, 768), BF16),
        ((256, 3072), BF16),
        ((3, 256, 1024), F32),
    )
    return pl.pallas_call(
        encoder_forward_kernel,
        out_shape=(jax.ShapeDtypeStruct((256, 768), BF16), jax.ShapeDtypeStruct((16, 1024), F32))
        + tuple(jax.ShapeDtypeStruct(*shape) for shape in shapes),
        in_specs=[smem_spec()] + [vmem_spec()] * 4 + [any_spec()] * 5,
        out_specs=(vmem_spec(),) * 2 + (any_spec(),) * len(shapes),
        scratch_shapes=[pltpu.VMEM(*shape) for shape in shapes]
        + [
            pltpu.VMEM((256, 768), F32),
            pltpu.VMEM(attend.shape, BF16),
            pltpu.VMEM(merging.shape, BF16),
            pltpu.VMEM(expand.shape, BF16),
            pltpu.VMEM(shrink.shape, BF16),
            pltpu.VMEM((768, 256), F32),
            pltpu.SemaphoreType.DMA((11,)),
            pltpu.SemaphoreType.DMA((len(shapes),)),
        ],
        compiler_params=pltpu.CompilerParams(vmem_limit_bytes=60 * 2**20),
        name="encoder_forward",
    )(sizes, gains, shifts, biases, inner[None], tokens, attend, merging, expand, shrink)


def decoder_kernel(
    reduce, sizes, distance, slots, frequency, sent, biases, mask_token, gains, shifts, inner,
    cotangent, entry_far, attend_far, merging_far, expand_far, shrink_far,
    summed, rest, vectors, encoded_grad, *refs,
):
    (
        table, start, normed, mixed, turned, probs, flipped, context, normed_two, active,
        before_grad, go_low, attention_low, context_grad, delta, mixed_grad, target, masked_keys,
        entry_weight, attend, merging, expand, shrink, load_sem,
    ) = refs[:24]
    pack = lax.axis_index("section")
    if reduce:
        mine, partner = neighbours()
        greet(partner)
        engine = reducer(DECODER_PLAN, mine, partner, summed, refs[24:])
        put = engine.put
    else:
        put = put_into(summed)
    put_rest = put_into(rest)
    loads = fetch(
        [
            (entry_far, entry_weight),
            (attend_far, attend),
            (cotangent.at[pack], target),
            (merging_far, merging),
            (expand_far, expand),
            (shrink_far, shrink),
        ],
        load_sem,
    )
    tiles = start.shape[0] // TILE
    vectors[...] = jnp.zeros_like(vectors)
    large = sizes[pack, 0] == 1024

    def add_row(row, value):
        vectors[row : row + 1, :] += value

    positions = iota((32, 128), 0).astype(F32)
    for chip in range(4):
        spacing = distance[pack, chip].astype(F32) / 16.0
        angle = positions * (spacing * frequency[...])
        table[0, chip] = jnp.sin(angle)
        table[1, chip] = jnp.cos(angle)
    loads[0].wait()
    entry = low(dot(sent[...], entry_weight[...]) + biases[0:1])
    loads[1].wait()

    blocks = start.shape[0] // BLOCK

    def slot_chip(tile, size):
        return chip_of(iota((size, 1), 0) + tile * size, sizes, pack)

    def validity(tile, size):
        return (slot_chip(tile, size) < 4).astype(F32)

    def spread_of(tile):
        return (slots[pl.ds(pack, 1)] == iota((TILE, TILE), 0) + tile * TILE).astype(F32)

    def encoding_of(tile):
        pieces = []
        for kind in range(2):
            wave = table[kind, 0, aligned(tile * 8, 8, 8)]
            big = jnp.broadcast_to(wave[:, None], (8, 32, 128)).reshape(TILE, 128)
            wave = table[kind, tile, 0:16]
            own = jnp.broadcast_to(wave[:, None], (16, 16, 128)).reshape(TILE, 128)
            pieces.append(jnp.where(large, big, own))
        for kind in range(2):
            wave = table[kind, 0]
            big = jnp.broadcast_to(wave[None], (8, 32, 128)).reshape(TILE, 128)
            wave = table[kind, tile, 0:16]
            own = jnp.broadcast_to(wave[None], (16, 16, 128)).reshape(TILE, 128)
            pieces.append(jnp.where(large, big, own))
        return jnp.concatenate(pieces, axis=1)

    @pl.loop(0, tiles)
    def _(tile):
        rows = rows_of(tile)
        valid = validity(tile, TILE)
        spread = spread_of(tile)
        fill = valid * (1.0 - jnp.sum(spread, axis=1, keepdims=True))
        hidden = dot(low(spread), entry) + fill * mask_token[...] + encoding_of(tile) * valid
        start[rows] = hidden
        add_row(12, row_sum(valid * hidden * hidden))
        add_row(16, row_sum(valid))
        unit, _ = standardize(hidden)
        norm = low(unit * gains[0:1] + shifts[0:1])
        normed[rows] = norm
        mix = dot(norm, attend[...])
        mix_low = low(mix)
        mixed[rows] = mix_low
        turned[:, rows] = low(mix[:, 256:].T)
        lane = iota((TILE, 128), 1)
        other = (lane % 64 < 5) & (lane % 64 != slot_chip(tile, TILE))
        other = jnp.where(other, NEGATIVE, 0.0).astype(BF16)
        for head in range(4):
            lanes = slice(256 + head // 2 * 128, 384 + head // 2 * 128)
            masked_keys[head, rows] = jnp.where(lane // 64 == head % 2, mix_low[:, lanes], other)

    @pl.loop(0, 2 * tiles)
    def _(step):
        pair, tile = step // tiles, step % tiles
        rows = rows_of(tile)
        lane = iota((TILE, 128), 1)
        chosen = (lane % 64 == slot_chip(tile, TILE)).astype(F32).astype(BF16)
        for half in range(2):
            query = jnp.where(lane // 64 == half, mixed[rows, pair_lanes(pair)] * BF16(0.125), chosen)
            scores = dot_nt(masked_keys[pair * 2 + half], query)
            expos = jnp.exp(scores - jnp.max(scores, axis=0, keepdims=True))
            prob = low(expos * (1.0 / jnp.sum(expos, axis=0, keepdims=True)))
            probs[pair * 2 + half, :, rows] = prob
            flipped[head_rows(pair, half), rows] = dot(turned[head_rows(pair, half, 256)], prob)

    for copy in loads[2:]:
        copy.wait()

    @pl.loop(0, blocks)
    def _(tile):
        rows = rows_of(tile, BLOCK)
        valid = validity(tile, BLOCK)
        mingled = low(flipped[:, rows].T)
        context[rows] = mingled
        attention = dot(mingled, merging[...]) + biases[1:2]
        add_row(13, row_sum(valid * attention * attention))
        unit, _ = standardize(start[rows] + attention)
        norm = low(unit * gains[1:2] + shifts[1:2])
        normed_two[rows] = norm
        go = target[rows] * valid
        go_below = low(go)
        go_low[rows] = go_below
        add_row(2, row_sum(go))
        for part in range(8):
            cols = slice(part * 256, part * 256 + 256)
            value, slope = gelu_pair(dot(norm, expand[:, cols]) + inner[:, cols])
            active[rows, cols] = low(value)
            grad = low(slope * dot_nt(go_below, shrink[cols]))
            before_grad[rows, cols] = grad
            lanes = slice(part % 2 * 256, part % 2 * 256 + 256)
            vectors[8 + part // 2 : 9 + part // 2, lanes] += row_sum(grad.astype(F32))

    if reduce:
        await_greetings()
    for part in range(2):
        cols = slice(part * 256, part * 256 + 256)
        store_packed(put, part * 16, DECODER_EXPAND, dot_tn(normed_two[:, cols], before_grad[...]))
    if reduce:
        engine.send(2048)

    @pl.loop(0, 8)
    def _(part):
        cols = aligned(part * 256, 256, 256)
        store_packed(put, part * 4, DECODER_SHRINK, dot_tn(active[:, cols], go_low[...]))

    if reduce:
        engine.send(4096)

    @pl.loop(0, tiles)
    def _(tile):
        rows = rows_of(tile)
        valid = validity(tile, TILE)
        center = start[rows] + (dot(context[rows], merging[...]) + biases[1:2])
        unit, inverse = standardize(center)
        feed = dot(active[rows], shrink[...]) + biases[2:3]
        add_row(14, row_sum(valid * feed * feed))
        output = center + feed
        add_row(15, row_sum(valid * output * output))
        norm_grad = dot_nt(before_grad[rows], expand[...])
        add_row(5, row_sum(norm_grad * unit))
        add_row(7, row_sum(norm_grad))
        grad = target[rows] * valid + norm_back(unit, inverse, gains[1:2], norm_grad)
        target[rows] = grad
        add_row(1, row_sum(grad))
        below = low(grad)
        attention_low[rows] = below
        outer = low(dot_nt(below, merging[...]))
        context_grad[rows] = outer
        product = (outer.astype(F32) * flipped[:, rows].T).T
        for head in range(4):
            delta[head, :, rows] = row_sum(product[head * 64 : head * 64 + 64])
        if reduce:
            engine.turn(tile)

    for part in range(2):
        cols = slice(part * 256, part * 256 + 256)
        store_packed(put, part * 16, DECODER_MERGE, dot_tn(attention_low[:, cols], context[...]))
        shards = slice(part * 16, part * 16 + 16)
        put(shards, 4352, jnp.zeros((16, 16, DECODER_PLAN.chunks * DECODER_PLAN.span - 4352), F32))
    if reduce:
        engine.send(DECODER_PLAN.chunks * DECODER_PLAN.span)

    flipped[...] = jnp.zeros_like(flipped)

    @pl.loop(0, 2 * tiles)
    def _(step):
        pair, tile = step // tiles, step % tiles
        rows = rows_of(tile)
        lanes = pair_lanes(pair)
        values = mixed[rows, pair_lanes(pair, 512)]
        raws, probabilities, queries, outers = [], [], [], []
        for half in range(2):
            prob = probs[pair * 2 + half, rows]
            outer = only(context_grad[:, lanes], half)
            raw = low(prob.astype(F32) * (dot_nt(values, outer) - delta[pair * 2 + half]))
            flipped[head_rows(pair, half)] += dot(turned[head_rows(pair, half), rows], raw)
            raws.append(raw)
            probabilities.append(prob)
            outers.append(outer)
            queries.append(only(mixed[:, lanes], half))
        key_grad = dot(jnp.concatenate(raws, axis=1), jnp.concatenate(queries, axis=0))
        mixed_grad[rows, pair_lanes(pair, 256)] = low(key_grad * 0.125)
        value_grad = dot(jnp.concatenate(probabilities, axis=1), jnp.concatenate(outers, axis=0))
        mixed_grad[rows, pair_lanes(pair, 512)] = low(value_grad)
        if reduce:
            engine.turn(tiles + step)

    def last(tile, entry_grad):
        rows = rows_of(tile)
        mixed_grad[rows, 0:256] = low(flipped[:, rows].T * 0.125)
        norm_grad = dot_nt(mixed_grad[rows], attend[...])
        unit, inverse = standardize(start[rows])
        add_row(4, row_sum(norm_grad * unit))
        add_row(6, row_sum(norm_grad))
        grad = target[rows] + norm_back(unit, inverse, gains[0:1], norm_grad)
        spread = spread_of(tile)
        fill = validity(tile, TILE) * (1.0 - jnp.sum(spread, axis=1, keepdims=True))
        add_row(3, row_sum(fill * grad))
        if reduce:
            engine.turn(3 * tiles + tile)
        return entry_grad + dot_tn(low(spread), low(grad))

    entry_grad = lax.fori_loop(0, tiles, last, jnp.zeros((TILE, 512), F32))
    add_row(0, row_sum(entry_grad))
    entry_low = low(entry_grad)
    encoded_grad[...] = low(dot_nt(entry_low, entry_weight[...]))
    store_packed(put_rest, 0, ENTRY, dot_tn(sent[...], entry_low))

    @pl.loop(0, 2)
    def _(part):
        cols = aligned(part * 256, 256, 256)
        store_packed(put_rest, part * 16, DECODER_ATTEND, dot_tn(normed[:, cols], mixed_grad[...]))

    if reduce:
        engine.close()


def decoder_call(
    reduce, sizes, distance, slots, sent, cotangent, entry_weight, biases, mask_token,
    gains, shifts, attend, merging, expand, inner, shrink,
):
    length = cotangent.shape[1]
    width = 512
    frequency = np.exp(-np.log(10000.0) * np.arange(width // 4) / (width // 4)).astype(np.float32)
    if reduce:
        summed = jax.ShapeDtypeStruct((DECODER_PLAN.chunks, 16, DECODER_PLAN.span), F32)
        extra = reducer_scratch(DECODER_PLAN)
        params = dict(collective_id=1, has_side_effects=True)
    else:
        summed = jax.ShapeDtypeStruct((DECODER_PLAN.chunks, 2, 16, 16, DECODER_PLAN.span), BF16)
        extra = []
        params = dict()
    return pl.pallas_call(
        functools.partial(decoder_kernel, reduce),
        out_shape=(
            summed,
            jax.ShapeDtypeStruct((1, 2, 16, 16, UNIT), BF16),
            jax.ShapeDtypeStruct((24, width), F32),
            jax.ShapeDtypeStruct((256, 768), BF16),
        ),
        in_specs=[smem_spec()] * 2 + [vmem_spec()] * 8 + [any_spec()] * 6,
        out_specs=(vmem_spec(),) * 4,
        scratch_shapes=[
            pltpu.VMEM((2, 4, 32, 128), F32),
            pltpu.VMEM((length, width), F32),
            pltpu.VMEM((length, width), BF16),
            pltpu.VMEM((length, 768), BF16),
            pltpu.VMEM((512, length), BF16),
            pltpu.VMEM((4, length, length), BF16),
            pltpu.VMEM((256, length), F32),
            pltpu.VMEM((length, 256), BF16),
            pltpu.VMEM((length, width), BF16),
            pltpu.VMEM((length, 2048), BF16),
            pltpu.VMEM((length, 2048), BF16),
            pltpu.VMEM((length, width), BF16),
            pltpu.VMEM((length, width), BF16),
            pltpu.VMEM((length, 256), BF16),
            pltpu.VMEM((4, 1, length), F32),
            pltpu.VMEM((length, 768), BF16),
            pltpu.VMEM((length, width), F32),
            pltpu.VMEM((4, length, 128), BF16),
            pltpu.VMEM(entry_weight.shape, BF16),
            pltpu.VMEM(attend.shape, BF16),
            pltpu.VMEM(merging.shape, BF16),
            pltpu.VMEM(expand.shape, BF16),
            pltpu.VMEM(shrink.shape, BF16),
            pltpu.SemaphoreType.DMA((6,)),
        ]
        + extra,
        compiler_params=pltpu.CompilerParams(vmem_limit_bytes=63 * 2**20, **params),
        name="decoder_block",
    )(
        sizes, distance, slots, jnp.asarray(frequency)[None], sent, biases, mask_token[None], gains, shifts,
        inner[None], cotangent, entry_weight, attend, merging, expand, shrink,
    )


def encoder_backward_kernel(
    reduce, encoded_grad, sums, decoder_vectors, gains, tokens, rest, attend_far, merging_far, expand_far,
    shrink_far, normed_far, mixed_far, turned_far, probs_far, context_far, middle_far, normed_two_far, active_far,
    slope_far, summed, tail_summed, vectors, tokens_grad, *refs,
):
    if reduce:
        decoder_sums, arrived = refs[:2]
        refs = refs[2:]
    (
        hidden, attend, merging, expand, shrink, normed, mixed, turned, probs, context, middle, normed_two, active,
        slope, before_grad, norm_sum, attention_low, context_grad, key_grad, query_turned, mixed_grad, active_turned,
        flipped, inner_sum, load_sem, part_sem,
    ) = refs[:26]
    pack = lax.axis_index("section")

    def part_loads(part):
        cols = aligned(part * 1024, 1024, 1024)
        slot = part % 2
        return [
            pltpu.make_async_copy(expand_far.at[:, cols], expand.at[slot], part_sem.at[slot, 0]),
            pltpu.make_async_copy(shrink_far.at[cols], shrink.at[slot], part_sem.at[slot, 1]),
            pltpu.make_async_copy(slope_far.at[part], slope.at[slot], part_sem.at[slot, 2]),
        ]

    if reduce:
        (
            decoder_total, encoder_total, decoder_got, encoder_got, payload,
            own_sem, small_send, small_recv, pay_send, pay_recv, small_load,
        ) = refs[26:37]
        mine, partner = neighbours()
        greet(partner)
        engine = reducer(ENCODER_PLAN, mine, partner, summed, refs[37:68])
        tail = reducer(TAIL_PLAN, mine, partner, tail_summed, refs[68:])
        put_tail = tail.put
        first_own = fetch(
            [
                pair
                for pair in (
                    (rest.at[0, 1 - mine["c"]], engine.staging.at[0]),
                    (rest.at[0, mine["c"]], engine.own.at[0]),
                )
            ],
            own_sem,
        )
        decoder_load = pltpu.make_async_copy(decoder_vectors, decoder_total.at[0], small_load)
        decoder_load.start()
    else:
        put_tail = put_into(tail_summed)
    early = pltpu.make_async_copy(active_far, active, load_sem.at[10])
    early.start()
    for copy in part_loads(0):
        copy.start()
    if reduce:
        for copy in first_own:
            copy.wait()
        await_greetings()
        engine.first_copy(0).start()
    loads = fetch(
        [
            (normed_two_far, normed_two),
            (middle_far, middle),
            (merging_far, merging),
            (context_far, context),
            (mixed_far, mixed),
            (probs_far, probs),
            (turned_far.at[0:768], turned),
            (normed_far, normed),
            (attend_far, attend),
            (tokens.at[pack], hidden),
        ],
        load_sem,
    )
    for copy in part_loads(1):
        copy.start()
    vectors[...] = sums[...]
    go_low = encoded_grad[...]
    go = go_low.astype(F32)
    vectors[1:2, :768] = row_sum(go)
    norm_sum[...] = jnp.zeros_like(norm_sum)

    def unit_grad(unit, place, pieces):
        put = engine.put_unit(unit) if reduce else put_unit_into(summed, unit)
        for first, value in pieces:
            store_packed(put, first, (0,) + place[1:], value)
        if reduce:
            engine.first_copy(unit).start()

    def shrink_start():
        early.wait()
        for piece in range(4):
            rows = slice(piece * 768, piece * 768 + 768)
            active_turned[rows] = active[:, rows].T

    def shrink_grad(part):
        cols = aligned(part * 256, 256, 256)
        pieces = []
        for piece in range(4):
            rows = slice(piece * 768, piece * 768 + 768)
            pieces.append((piece * 8, dot(active_turned[rows], encoded_grad[:, cols])))
        unit_grad(1 + part, ENCODER_SHRINK[0], pieces)

    def hidden_layer(part):
        for copy in part_loads(part):
            copy.wait()
        slot = part % 2
        grad = low(slope[slot] * dot_nt(encoded_grad[...], shrink[slot]))
        before_grad[...] = grad
        inner_sum[part] = row_sum(grad.astype(F32))
        norm_sum[...] += dot_nt(grad, expand[slot])

        @pl.when(part == 0)
        def _():
            for copy in part_loads(2):
                copy.start()

    def expand_grad(part):
        @pl.when(part == 0)
        def _():
            loads[0].wait()
            flipped[...] = normed_two[...].T

        unit_grad(4 + part, ENCODER_EXPAND[0], [(0, dot(flipped[...], before_grad[...]))])

    def middle_layer():
        loads[1].wait()
        loads[2].wait()
        for part in range(3):
            vectors[6 + part : 7 + part] = inner_sum[part]
        unit, inverse = standardize(middle[...])
        norm_grad = norm_sum[...]
        vectors[3:4, :768] = row_sum(norm_grad * unit)
        vectors[5:6, :768] = row_sum(norm_grad)
        grad = encoded_grad[...].astype(F32) + norm_back(unit, inverse, gains[1:2], norm_grad)
        vectors[0:1, :768] = row_sum(grad)
        tokens_grad[...] = grad
        below = low(grad)
        attention_low[...] = below
        context_grad[...] = low(dot_nt(below, merging[...]))
        for copy in loads[3:7]:
            copy.wait()

    def attention(first):
        @pl.loop(first, first + 2)
        def _(pair):
            lanes = pair_lanes(pair)
            values = mixed[:, pair_lanes(pair, 1536)]
            keys_total = jnp.zeros((TILE, 128), F32)
            values_total = jnp.zeros((TILE, 128), F32)
            for half in range(2):
                prob = probs[pair * 2 + half]
                outer = only(context_grad[:, lanes], half)
                query = only(mixed[:, lanes], half)
                wide = prob.astype(F32)
                grad = dot_nt(values, outer)
                raw = low(wide * (grad - jnp.sum(wide * grad, axis=0, keepdims=True)))
                keys_total = keys_total + dot(raw, query)
                values_total = values_total + dot(prob, outer)
                rows = head_rows(pair, half)
                query_turned[rows] = dot(turned[rows], raw)
            key_grad[0, :, lanes] = keys_total
            key_grad[1, :, lanes] = values_total

    def mixing():
        mixed_grad[:, 0:768] = low(query_turned[...].T * 0.125)
        mixed_grad[:, 768:1536] = low(key_grad[0] * 0.125)
        mixed_grad[:, 1536:2304] = low(key_grad[1])

    def attend_grad(part):
        @pl.when(part == 0)
        def _():
            loads[7].wait()
            flipped[...] = normed[...].T

        wide = aligned(part * 1024, 1024, 1024)
        unit_grad(7 + part, ENCODER_ATTEND[0], [(0, dot(flipped[...], mixed_grad[:, wide]))])

    def tail_grad():
        store_packed(put_tail, 0, ENCODER_ATTEND[2], dot(flipped[...], mixed_grad[:, 2048:2304]))
        store_packed(put_tail, 0, ENCODER_MERGE, dot_tn(attention_low[...], context[...]))
        if reduce:
            tail.send(UNIT)

    def input_layer():
        loads[8].wait()
        loads[9].wait()
        norm_grad = dot_nt(mixed_grad[...], attend[...])
        unit, inverse = standardize(hidden[...])
        vectors[2:3, :768] = row_sum(norm_grad * unit)
        vectors[4:5, :768] = row_sum(norm_grad)
        grad = tokens_grad[...] + norm_back(unit, inverse, gains[0:1], norm_grad)
        tokens_grad[...] = grad
        if reduce:
            payload[...] = low(grad)

    if not reduce:
        shrink_start()
        for part in range(3):
            shrink_grad(part)
        for part in range(3):
            hidden_layer(part)
            expand_grad(part)
        middle_layer()
        for first in (0, 2, 4):
            attention(first)
        mixing()
        for part in range(2):
            attend_grad(part)
        tail_grad()
        input_layer()
        return

    def exchange(source, piece):
        rows = aligned(piece * 32, 32, 32)
        return remote(source.at[rows], arrived.at[rows], pay_send.at[piece], pay_recv.at[piece], partner["x"])

    small_route = ("c",) + ROUTES[0]
    totals = ((decoder_total, decoder_got), (encoder_total, encoder_got))

    def small_copy(stage, kind):
        source, target = totals[kind]
        return remote(
            source.at[stage],
            target.at[stage],
            small_send.at[stage, kind],
            small_recv.at[stage, kind],
            partner[small_route[stage]],
        )

    def small_advance(stage):
        if stage == 0:
            encoder_total[0] = vectors[...]
        for kind in range(2):
            source, target = totals[kind]
            if stage > 0:
                small_copy(stage - 1, kind).wait_recv()
                source[stage] = source[stage - 1] + target[stage - 1]
            if stage < 5:
                small_copy(stage, kind).start()

    shrink_start()
    shrink_grad(0)
    decoder_load.wait()

    def attention_all():
        @pl.loop(0, 3)
        def _(step):
            attention(2 * step)

        mixing()

    def ending():
        tail_grad()
        input_layer()

    part = functools.partial
    works = {4: middle_layer, 5: attention_all, 7: ending}
    turns = ENCODER_PLAN.chunks + TAIL_PLAN.chunks + 4 * LAG
    works.update({8 + stage + max(0, stage - 1): part(small_advance, stage) for stage in range(6)})

    @pl.loop(0, turns)
    def _(number):
        engine.turn(number)
        tail.turn(number - ENCODER_PLAN.chunks)

        @pl.when(number <= 1)
        def _():
            shrink_grad(number + 1)

        @pl.when((number >= 2) & (number <= 4))
        def _():
            expand_grad(number - 2)

        @pl.when((number >= 1) & (number <= 3))
        def _():
            hidden_layer(number - 1)

        for position, work in works.items():
            pl.when(number == position)(work)

        @pl.when(number == 6)
        def _():
            @pl.loop(0, 2)
            def _(part):
                attend_grad(part)

        @pl.when((pack == 0) & (number < 8))
        def _():
            exchange(encoded_grad, number).start()

        @pl.when((pack == 1) & (number >= 8) & (number < 16))
        def _():
            exchange(payload, number - 8).start()

    for stage in range(5):
        for kind in range(2):
            small_copy(stage, kind).wait_send()
    for piece in range(8):
        exchange(payload, piece).wait()
    engine.close()
    tail.close()
    vectors[...] = encoder_total[5]
    decoder_sums[...] = decoder_total[5]


def encoder_backward_call(reduce, tokens, encoded_grad, sums, decoder_vectors, rest, kept, gains, attend, merging, expand, shrink):
    if reduce:
        summed = tuple(
            jax.ShapeDtypeStruct((plan.chunks, 16, plan.span), F32) for plan in (ENCODER_PLAN, TAIL_PLAN)
        )
        more = (
            jax.ShapeDtypeStruct(decoder_vectors.shape, F32),
            jax.ShapeDtypeStruct((256, 768), BF16),
        )
        more_specs = (vmem_spec(), any_spec())
        extra = [
            pltpu.VMEM((6,) + decoder_vectors.shape, F32),
            pltpu.VMEM((6,) + sums.shape, F32),
            pltpu.VMEM((5,) + decoder_vectors.shape, F32),
            pltpu.VMEM((5,) + sums.shape, F32),
            pltpu.VMEM((256, 768), BF16),
            pltpu.SemaphoreType.DMA((2,)),
            pltpu.SemaphoreType.DMA((5, 2)),
            pltpu.SemaphoreType.DMA((5, 2)),
            pltpu.SemaphoreType.DMA((8,)),
            pltpu.SemaphoreType.DMA((8,)),
            pltpu.SemaphoreType.DMA,
        ] + reducer_scratch(ENCODER_PLAN) + reducer_scratch(TAIL_PLAN)
        params = dict(collective_id=2, has_side_effects=True)
    else:
        summed = tuple(
            jax.ShapeDtypeStruct((plan.chunks, 2, 16, 16, plan.span), BF16) for plan in (ENCODER_PLAN, TAIL_PLAN)
        )
        more, more_specs, extra, params = (), (), [], dict()
    return pl.pallas_call(
        functools.partial(encoder_backward_kernel, reduce),
        out_shape=summed
        + (
            jax.ShapeDtypeStruct(sums.shape, F32),
            jax.ShapeDtypeStruct((256, 768), F32),
        )
        + more,
        in_specs=[vmem_spec()] * 2 + [any_spec(), vmem_spec()] + [any_spec()] * 15,
        out_specs=(vmem_spec(),) * 4 + more_specs,
        scratch_shapes=[
            pltpu.VMEM((256, 768), F32),
            pltpu.VMEM(attend.shape, BF16),
            pltpu.VMEM(merging.shape, BF16),
            pltpu.VMEM((2, 768, 1024), BF16),
            pltpu.VMEM((2, 1024, 768), BF16),
            pltpu.VMEM((256, 768), BF16),
            pltpu.VMEM((256, 2304), BF16),
            pltpu.VMEM((768, 256), BF16),
            pltpu.VMEM((12, 256, 256), BF16),
            pltpu.VMEM((256, 768), BF16),
            pltpu.VMEM((256, 768), F32),
            pltpu.VMEM((256, 768), BF16),
            pltpu.VMEM((256, 3072), BF16),
            pltpu.VMEM((2, 256, 1024), F32),
            pltpu.VMEM((256, 1024), BF16),
            pltpu.VMEM((256, 768), F32),
            pltpu.VMEM((256, 768), BF16),
            pltpu.VMEM((256, 768), BF16),
            pltpu.VMEM((2, 256, 768), F32),
            pltpu.VMEM((768, 256), F32),
            pltpu.VMEM((256, 2304), BF16),
            pltpu.VMEM((3072, 256), BF16),
            pltpu.VMEM((768, 256), BF16),
            pltpu.VMEM((3, 1, 1024), F32),
            pltpu.SemaphoreType.DMA((11,)),
            pltpu.SemaphoreType.DMA((2, 3)),
        ]
        + extra,
        compiler_params=pltpu.CompilerParams(vmem_limit_bytes=62 * 2**20, **params),
        name="encoder_backward",
    )(encoded_grad, sums, decoder_vectors, gains, tokens, rest, attend, merging, expand, shrink, *kept)


def unpack(packed, place):
    span = packed.shape[-1]

    def take(start, size):
        pieces = []
        while size:
            chunk, first = divmod(start, span)
            length = min(size, span - first)
            pieces.append(packed[chunk, ..., first : first + length])
            start, size = start + length, size - length
        return pieces[0] if len(pieces) == 1 else jnp.concatenate(pieces, axis=-1)

    offset, count, width = place
    pieces = [take(offset + i * width, width) for i in range(count // 16)]
    if count % 16:
        rest = take(offset + count // 16 * width, width // 2)
        pieces.append(jnp.concatenate([rest[..., :8, :], rest[..., 8:, :]], axis=-1))
    return pieces[0] if len(pieces) == 1 else jnp.concatenate(pieces, axis=-2)


def finish_kernel(
    decoder_summed_far, decoder_sums_far, encoder_sums_far, summed_far, tail_far, arrived_far, tokens_grad_far, encoded_grad_far,
    boundary, statistics, e_gains, e_shifts, e_biases, e_attend, e_merge, e_expand, e_inner, e_shrink,
    d_entry, d_biases, mask_grad, d_gains, d_shifts, d_attend, d_merge, d_expand, d_inner, d_shrink,
    decoder_summed, decoder_sums, encoder_sums, summed, tail, arrived, tokens_grad, encoded_grad, load_sem,
):
    section = lax.axis_index("section")
    loads = fetch(
        [
            (decoder_summed_far, decoder_summed),
            (decoder_sums_far, decoder_sums),
            (encoder_sums_far, encoder_sums),
            (summed_far, summed),
            (tail_far, tail),
            (arrived_far, arrived),
            (tokens_grad_far, tokens_grad),
            (encoded_grad_far, encoded_grad),
        ],
        load_sem,
    )
    number = section * lax.axis_size("dp") + lax.axis_index("dp")

    def own(rows, count):
        width = rows.shape[1]
        return pltpu.roll(rows, (width - number * count) % width, axis=1)[:, :count]

    def own_line(rows, count):
        return own(jnp.concatenate([rows[i : i + 1] for i in range(rows.shape[0])], axis=1), count)

    for copy in loads[:3]:
        copy.wait()
    lane = iota((1, 128), 1)
    values = jnp.zeros((1, 128), F32)
    for sums, width, first, count_row, base in ((encoder_sums, DE, 10, 14, 0), (decoder_sums, DD, 12, 16, 4)):
        scale = 1.0 / (sums[count_row : count_row + 1, 0:1] * width)
        for i in range(4):
            value = jnp.sum(sums[first + i : first + i + 1, :], axis=1, keepdims=True) * scale
            values = jnp.where(lane == base + i, value, values)
    statistics[...] = jnp.sqrt(values)[:, :8]
    rows = own(encoder_sums[0:8, :DE], 24)
    e_biases[...] = rows[0:2]
    e_gains[...] = rows[2:4]
    e_shifts[...] = rows[4:6]
    e_inner[...] = own_line(encoder_sums[6:9], 96)
    rows = own(decoder_sums[0:8], 16)
    d_biases[...] = rows[0:3]
    mask_grad[...] = rows[3:4]
    d_gains[...] = rows[4:6]
    d_shifts[...] = rows[6:8]
    d_inner[...] = own_line(decoder_sums[8:12], 64)

    d_merge[...] = unpack(decoder_summed, DECODER_MERGE)
    d_expand[...] = unpack(decoder_summed, DECODER_EXPAND)
    d_shrink[...] = unpack(decoder_summed, DECODER_SHRINK)
    loads[3].wait()
    loads[4].wait()
    d_entry[...] = unpack(summed, ENTRY)
    d_attend[...] = unpack(summed, DECODER_ATTEND)
    for target, places in ((e_expand, ENCODER_EXPAND), (e_attend, ENCODER_ATTEND), (e_shrink, ENCODER_SHRINK)):
        start = 0
        for place in places:
            source = tail if place is ENCODER_ATTEND[2] else summed
            target[:, start : start + place[2]] = unpack(source, place)
            start += place[2]
    e_merge[...] = unpack(tail, ENCODER_MERGE)
    for copy in loads[5:]:
        copy.wait()

    @pl.when(section == 0)
    def _():
        boundary[0, 0] = tokens_grad[...]
        boundary[0, 1] = arrived[...].astype(F32)

    @pl.when(section == 1)
    def _():
        boundary[0, 0] = arrived[...].astype(F32)
        boundary[0, 1] = encoded_grad[...].astype(F32)


def finish_call(*operands):
    shapes = (
        (1, 2, 256, 768), (1, 8), (2, 24), (2, 24), (2, 24), (24, 2304), (24, 768), (24, 3072), (1, 96), (96, 768),
        (24, 512), (3, 16), (1, 16), (2, 16), (2, 16), (16, 768), (16, 256), (16, 2048), (1, 64), (64, 512),
    )
    outs = list(
        pl.pallas_call(
            finish_kernel,
            out_shape=tuple(jax.ShapeDtypeStruct(shape, F32) for shape in shapes),
            in_specs=[any_spec()] * len(operands),
            out_specs=(vmem_spec(),) * len(shapes),
            scratch_shapes=[pltpu.VMEM(operand.shape, operand.dtype) for operand in operands]
            + [pltpu.SemaphoreType.DMA((len(operands),))],
            compiler_params=pltpu.CompilerParams(vmem_limit_bytes=60 * 2**20),
            name="finish",
        )(*operands)
    )
    for line in (1, 8, 12, 18):
        outs[line] = outs[line].reshape(-1)
    for turned in (6, 16):
        outs[turned] = outs[turned].T
    return tuple(outs)


def scatter_sum(member, share_dim):
    return lax.psum_scatter(
        member, ("section", "dp"), scatter_dimension=share_dim, tiled=True
    )


def finish_generic(decoder_part, part, tail, decoder_sums, encoder_sums, tokens_grad, encoded_grad):
    section = lax.axis_index("section")
    payload = jnp.where(section == 0, encoded_grad, low(tokens_grad))

    def whole(packed, *places):
        packed = jnp.swapaxes(packed, 1, 2).reshape(-1, 32, 16, packed.shape[-1])
        blocks = [unpack(packed, place).reshape(32 * place[1], place[2]) for place in places]
        return scatter_sum(jnp.concatenate(blocks, axis=1).astype(F32), 0)

    def line(value):
        return scatter_sum(value, value.ndim - 1)

    arrived = lax.ppermute(payload, "section", [(0, 1), (1, 0)]).astype(F32)
    boundary = jnp.where(
        section == 0,
        jnp.stack([tokens_grad, arrived]),
        jnp.stack([arrived, encoded_grad.astype(F32)]),
    )
    sums = jnp.concatenate(
        [jnp.sum(encoder_sums[10:14], axis=1), jnp.sum(decoder_sums[12:16], axis=1)]
    )
    sums, counts = lax.psum((sums, (encoder_sums[14, 0], decoder_sums[16, 0])), ("section", "dp"))
    scales = jnp.concatenate([jnp.full((4,), counts[0] * DE), jnp.full((4,), counts[1] * DD)])
    return (
        boundary[None],
        jnp.sqrt(sums / scales),
        line(encoder_sums[2:4, :DE]),
        line(encoder_sums[4:6, :DE]),
        line(encoder_sums[0:2, :DE]),
        jnp.concatenate([whole(part, *ENCODER_ATTEND[:2]), whole(tail, ENCODER_ATTEND[2])], axis=1),
        whole(tail, ENCODER_MERGE).T,
        whole(part, *ENCODER_EXPAND),
        line(encoder_sums[6:9].reshape(-1)),
        whole(part, *ENCODER_SHRINK),
        whole(decoder_part[1], ENTRY),
        line(decoder_sums[0:3]),
        line(decoder_sums[3]),
        line(decoder_sums[4:6]),
        line(decoder_sums[6:8]),
        whole(decoder_part[1], DECODER_ATTEND),
        whole(decoder_part[0], DECODER_MERGE).T,
        whole(decoder_part[0], DECODER_EXPAND),
        line(decoder_sums[8:12].reshape(-1)),
        whole(decoder_part[0], DECODER_SHRINK),
    )


def body(
    visible_tokens,
    cotangent,
    chip_sizes,
    ground_distance,
    visible_slots,
    encoder_gains,
    encoder_shifts,
    encoder_biases,
    encoder_attend,
    encoder_merge,
    encoder_expand,
    encoder_inner,
    encoder_shrink,
    decoder_entry,
    decoder_biases,
    mask_token,
    decoder_gains,
    decoder_shifts,
    decoder_attend,
    decoder_merge,
    decoder_widen_weight,
    decoder_inner,
    decoder_shrink,
):
    reduce = (lax.axis_size("section"), lax.axis_size("dp")) == (2, 16)
    sent, sums, *kept = encoder_forward_call(
        chip_sizes, visible_tokens, encoder_gains, encoder_shifts, encoder_biases,
        encoder_attend, encoder_merge, encoder_expand, encoder_inner, encoder_shrink,
    )
    decoder_summed, rest, decoder_vectors, encoded_grad = decoder_call(
        reduce, chip_sizes, ground_distance, visible_slots, sent, cotangent, decoder_entry, decoder_biases, mask_token,
        decoder_gains, decoder_shifts, decoder_attend, decoder_merge, decoder_widen_weight, decoder_inner,
        decoder_shrink,
    )
    summed, tail, encoder_sums, tokens_grad, *more = encoder_backward_call(
        reduce, visible_tokens, encoded_grad, sums, decoder_vectors, rest, kept,
        encoder_gains, encoder_attend, encoder_merge, encoder_expand, encoder_shrink,
    )
    if reduce:
        decoder_sums, arrived = more
        return finish_call(
            decoder_summed, decoder_sums, encoder_sums, summed, tail, arrived, tokens_grad, encoded_grad
        )
    return finish_generic(
        (decoder_summed, rest), summed, tail, decoder_vectors, encoder_sums, tokens_grad, encoded_grad
    )


def solution(mesh):
    in_specs = (
        P("dp", None, None),
        P("dp", None, None),
        P("dp", None),
        P("dp", None),
        P("dp", None),
        P(),
        P(),
        P(),
        P(),
        P(),
        P(),
        P(),
        P(),
        P(),
        P(),
        P(),
        P(),
        P(),
        P(),
        P(),
        P(),
        P(),
        P(),
    )
    out_specs = (
        P("section", "dp", None, None),
        P(),
        P(None, ("section", "dp")),
        P(None, ("section", "dp")),
        P(None, ("section", "dp")),
        P(("section", "dp"), None),
        P(None, ("section", "dp")),
        P(("section", "dp"), None),
        P(("section", "dp")),
        P(("section", "dp"), None),
        P(("section", "dp"), None),
        P(None, ("section", "dp")),
        P(("section", "dp")),
        P(None, ("section", "dp")),
        P(None, ("section", "dp")),
        P(("section", "dp"), None),
        P(None, ("section", "dp")),
        P(("section", "dp"), None),
        P(("section", "dp")),
        P(("section", "dp"), None),
    )
    return jax.shard_map(body, mesh=mesh, in_specs=in_specs, out_specs=out_specs, check_vma=False)
```

profile of v0, /device:TPU:0, one launch (start us, length us, event | category | flops | bytes accessed | tf_op | source)
XLA Modules:
  0.0 175.4 jit_solution(6738766854967201637)
XLA Ops:
  0.7 13.5 %encoder_forward.1 = (bf16[256,768]{1,0:T(8,128)(2,1)}, f32[16,1024]{1,0:T(8,128)}, bf16[256,768]{1,0:T(8,128)(2,1)}, bf16[256,2304]{1,0:T(8,128)(2,1)}, bf16[15...) custom-call(s32[2,4]{1,0:T(2,128)} %sizes.3, ...), custom_call_target="tpu_custom_call" | custom-call | tf_op jit(solution)/shard_map/encoder_forward/pallas_call | solution.py:468
  14.1 75.1 %decoder_block.1 = (f32[7,16,640]{2,1,0:T(8,128)}, bf16[1,2,16,16,1536]{4,3,2,1,0:T(8,128)(2,1)}, f32[24,512]{1,0:T(8,128)}, bf16[256,768]{1,0:T(8,128)(2,1)}) custom-call(s32[2,4]{1,0:T(2,128)} %sizes.3, s32[2,4]{1,0:T(2,128)} %distance.1, s32[2,256]{1,0:T(2,128)} %slots.1, f32[1,128]{1,0:T(1,128)} %constant.8.frequency, ...), custom_call_target="tpu_custom_call" | custom-call | tf_op jit(solution)/shard_map/decoder_block/pallas_call | solution.py:749
  89.3 82.4 %encoder_backward.1 = (f32[9,16,1536]{2,1,0:T(8,128)}, f32[2,16,768]{2,1,0:T(8,128)}, f32[16,1024]{1,0:T(8,128)}, f32[256,768]{1,0:T(8,128)}, f32[24,512]{1,0:T(8,128)}, /*index=5*/bf16[256,768]{1,0:T(8,128)(2,1)}) custom-call(bf16[256,768]{1,0:T(8,128)(2,1)} %get-tuple-element.63.encoded_grad.encoded_grad_far, f32[16,1024]{1,0:T(8,128)} %get-tuple-element.64.sums, ...), custom_call_target="tpu_custom_call" | custom-call | tf_op jit(solution)/shard_map/encoder_backward/pallas_call | solution.py:1127
  171.7 3.6 %finish.1 = (f32[1,2,256,768]{3,2,1,0:T(8,128)}, f32[1,8]{1,0:T(1,128)}, f32[2,24]{1,0:T(2,128)}, f32[2,24]{1,0:T(2,128)}, f32[2,24]{1,0:T(2,128)}, /*index=5*/f...) custom-call(f32[7,16,640]{2,1,0:T(8,128)} %get-tuple-element.62.deco, ...), custom_call_target="tpu_custom_call" | custom-call | tf_op jit(solution)/shard_map/finish/pallas_call | solution.py:1276
where the time goes:
time: 176 us; the launch traced here: 175 us
  Pallas kernels  175 us (99%)
    pallas_call x1, Pallas kernels, encoder_backward_call(): pl.pallas_call(functools.partial(encoder_backward_kernel, reduce), out_sh...  82.4 us
    pallas_call x1, Pallas kernels, decoder_call(): pl.pallas_call(functools.partial(decoder_kernel, reduce), out_shape=(summ...  75.1 us
    pallas_call x1, Pallas kernels, encoder_forward_call(): pl.pallas_call(encoder_forward_kernel, out_shape=(jax.ShapeDtypeStruct((2...  13.5 us
    pallas_call x1, Pallas kernels, finish_call(): pl.pallas_call(finish_kernel, out_shape=tuple((jax.ShapeDtypeStruct(shape...  3.58 us

commit v1 on v0

--- a/solution.py
+++ b/solution.py
@@ -21,7 +21,7 @@
 ROUTES = (("x", "y", "z1", "z2"), ("y", "x", "z1", "z2"), ("z1", "z2", "x", "y"))
 UNIT = 1536
 LAG = 2
-DECODER_PLAN = types.SimpleNamespace(widths=(2, 2, 1), chunks=7, slots=7, ring=3, span=640)
+DECODER_PLAN = types.SimpleNamespace(widths=(3, 4, 2), chunks=4, slots=4, ring=3, span=1152)
 ENCODER_PLAN = types.SimpleNamespace(widths=(3, 6, 3), chunks=9, slots=3, ring=3, span=1536)
 TAIL_PLAN = types.SimpleNamespace(widths=(2, 3, 1), chunks=2, slots=2, ring=2, span=768)
 
@@ -352,8 +352,8 @@
 
 
 def encoder_forward_kernel(
-    sizes, gains, shifts, biases, inner, tokens, attend_far, merging_far, expand_far, shrink_far,
-    sent, vectors, *refs,
+    sizes, distance, frequency, gains, shifts, biases, inner, tokens, attend_far, merging_far, expand_far,
+    shrink_far, sent, vectors, table, *refs,
 ):
     far = refs[:9]
     normed, mixed, turned, probs, context, middle, normed_two, active, slope = refs[9:18]
@@ -378,6 +378,12 @@
             saves.append(copy)
 
     vectors[...] = jnp.zeros_like(vectors)
+    positions = iota((32, 128), 0).astype(F32)
+    for chip in range(4):
+        spacing = distance[pack, chip].astype(F32) / 16.0
+        angle = positions * (spacing * frequency[...])
+        table[0, chip] = jnp.sin(angle)
+        table[1, chip] = jnp.cos(angle)
     key_chip = chip_of(4 * iota((TILE, 1), 0), sizes, pack)
     own_chip = chip_of(4 * iota((1, TILE), 1), sizes, pack)
     valid = (key_chip < 4).astype(F32)
@@ -453,7 +459,8 @@
         copy.wait()
 
 
-def encoder_forward_call(sizes, tokens, gains, shifts, biases, attend, merging, expand, inner, shrink):
+def encoder_forward_call(sizes, distance, tokens, gains, shifts, biases, attend, merging, expand, inner, shrink):
+    frequency = np.exp(-np.log(10000.0) * np.arange(DD // 4) / (DD // 4)).astype(np.float32)
     shapes = (
         ((256, 768), BF16),
         ((256, 2304), BF16),
@@ -467,10 +474,14 @@
     )
     return pl.pallas_call(
         encoder_forward_kernel,
-        out_shape=(jax.ShapeDtypeStruct((256, 768), BF16), jax.ShapeDtypeStruct((16, 1024), F32))
+        out_shape=(
+            jax.ShapeDtypeStruct((256, 768), BF16),
+            jax.ShapeDtypeStruct((16, 1024), F32),
+            jax.ShapeDtypeStruct((2, 4, 32, 128), F32),
+        )
         + tuple(jax.ShapeDtypeStruct(*shape) for shape in shapes),
-        in_specs=[smem_spec()] + [vmem_spec()] * 4 + [any_spec()] * 5,
-        out_specs=(vmem_spec(),) * 2 + (any_spec(),) * len(shapes),
+        in_specs=[smem_spec()] * 2 + [vmem_spec()] * 5 + [any_spec()] * 5,
+        out_specs=(vmem_spec(),) * 3 + (any_spec(),) * len(shapes),
         scratch_shapes=[pltpu.VMEM(*shape) for shape in shapes]
         + [
             pltpu.VMEM((256, 768), F32),
@@ -484,24 +495,27 @@
         ],
         compiler_params=pltpu.CompilerParams(vmem_limit_bytes=60 * 2**20),
         name="encoder_forward",
-    )(sizes, gains, shifts, biases, inner[None], tokens, attend, merging, expand, shrink)
+    )(
+        sizes, distance, jnp.asarray(frequency)[None], gains, shifts, biases, inner[None], tokens, attend, merging,
+        expand, shrink,
+    )
 
 
 def decoder_kernel(
-    reduce, sizes, distance, slots, frequency, sent, biases, mask_token, gains, shifts, inner,
+    reduce, sizes, slots, table, sent, biases, mask_token, gains, shifts, inner,
     cotangent, entry_far, attend_far, merging_far, expand_far, shrink_far,
     summed, rest, vectors, encoded_grad, *refs,
 ):
     (
-        table, start, normed, mixed, turned, probs, flipped, context, normed_two, active,
+        start, normed, mixed, turned, probs, flipped, context, normed_two, active,
         before_grad, go_low, attention_low, context_grad, delta, mixed_grad, target, masked_keys,
         entry_weight, attend, merging, expand, shrink, load_sem,
-    ) = refs[:24]
+    ) = refs[:23]
     pack = lax.axis_index("section")
     if reduce:
         mine, partner = neighbours()
         greet(partner)
-        engine = reducer(DECODER_PLAN, mine, partner, summed, refs[24:])
+        engine = reducer(DECODER_PLAN, mine, partner, summed, refs[23:])
         put = engine.put
     else:
         put = put_into(summed)
@@ -524,12 +538,6 @@
     def add_row(row, value):
         vectors[row : row + 1, :] += value
 
-    positions = iota((32, 128), 0).astype(F32)
-    for chip in range(4):
-        spacing = distance[pack, chip].astype(F32) / 16.0
-        angle = positions * (spacing * frequency[...])
-        table[0, chip] = jnp.sin(angle)
-        table[1, chip] = jnp.cos(angle)
     loads[0].wait()
     entry = low(dot(sent[...], entry_weight[...]) + biases[0:1])
     loads[1].wait()
@@ -666,7 +674,7 @@
         for head in range(4):
             delta[head, :, rows] = row_sum(product[head * 64 : head * 64 + 64])
         if reduce:
-            engine.turn(tile)
+            engine.turn(tile - 1)
 
     for part in range(2):
         cols = slice(part * 256, part * 256 + 256)
@@ -699,7 +707,7 @@
         value_grad = dot(jnp.concatenate(probabilities, axis=1), jnp.concatenate(outers, axis=0))
         mixed_grad[rows, pair_lanes(pair, 512)] = low(value_grad)
         if reduce:
-            engine.turn(tiles + step)
+            engine.turn(tiles - 1 + step)
 
     def last(tile, entry_grad):
         rows = rows_of(tile)
@@ -713,7 +721,7 @@
         fill = validity(tile, TILE) * (1.0 - jnp.sum(spread, axis=1, keepdims=True))
         add_row(3, row_sum(fill * grad))
         if reduce:
-            engine.turn(3 * tiles + tile)
+            engine.turn(3 * tiles - 1 + tile)
         return entry_grad + dot_tn(low(spread), low(grad))
 
     entry_grad = lax.fori_loop(0, tiles, last, jnp.zeros((TILE, 512), F32))
@@ -732,12 +740,11 @@
 
 
 def decoder_call(
-    reduce, sizes, distance, slots, sent, cotangent, entry_weight, biases, mask_token,
+    reduce, sizes, slots, table, sent, cotangent, entry_weight, biases, mask_token,
     gains, shifts, attend, merging, expand, inner, shrink,
 ):
     length = cotangent.shape[1]
     width = 512
-    frequency = np.exp(-np.log(10000.0) * np.arange(width // 4) / (width // 4)).astype(np.float32)
     if reduce:
         summed = jax.ShapeDtypeStruct((DECODER_PLAN.chunks, 16, DECODER_PLAN.span), F32)
         extra = reducer_scratch(DECODER_PLAN)
@@ -754,10 +761,9 @@
             jax.ShapeDtypeStruct((24, width), F32),
             jax.ShapeDtypeStruct((256, 768), BF16),
         ),
-        in_specs=[smem_spec()] * 2 + [vmem_spec()] * 8 + [any_spec()] * 6,
+        in_specs=[smem_spec()] + [vmem_spec()] * 8 + [any_spec()] * 6,
         out_specs=(vmem_spec(),) * 4,
         scratch_shapes=[
-            pltpu.VMEM((2, 4, 32, 128), F32),
             pltpu.VMEM((length, width), F32),
             pltpu.VMEM((length, width), BF16),
             pltpu.VMEM((length, 768), BF16),
@@ -786,7 +792,7 @@
         compiler_params=pltpu.CompilerParams(vmem_limit_bytes=63 * 2**20, **params),
         name="decoder_block",
     )(
-        sizes, distance, slots, jnp.asarray(frequency)[None], sent, biases, mask_token[None], gains, shifts,
+        sizes, slots, table, sent, biases, mask_token[None], gains, shifts,
         inner[None], cotangent, entry_weight, attend, merging, expand, shrink,
     )
 
@@ -1370,12 +1376,12 @@
     decoder_shrink,
 ):
     reduce = (lax.axis_size("section"), lax.axis_size("dp")) == (2, 16)
-    sent, sums, *kept = encoder_forward_call(
-        chip_sizes, visible_tokens, encoder_gains, encoder_shifts, encoder_biases,
+    sent, sums, table, *kept = encoder_forward_call(
+        chip_sizes, ground_distance, visible_tokens, encoder_gains, encoder_shifts, encoder_biases,
         encoder_attend, encoder_merge, encoder_expand, encoder_inner, encoder_shrink,
     )
     decoder_summed, rest, decoder_vectors, encoded_grad = decoder_call(
-        reduce, chip_sizes, ground_distance, visible_slots, sent, cotangent, decoder_entry, decoder_biases, mask_token,
+        reduce, chip_sizes, visible_slots, table, sent, cotangent, decoder_entry, decoder_biases, mask_token,
         decoder_gains, decoder_shifts, decoder_attend, decoder_merge, decoder_widen_weight, decoder_inner,
         decoder_shrink,
     )

time: 176 us -> 178 us (1.011)
  Pallas kernels: 175 us -> 177 us
    pallas_call x1, Pallas kernels: 75.1 us -> 78.1 us  [decoder_call(): pl.pallas_call(functools.partial(decoder_kernel, reduce), out_shape=(summ...]
where the time goes in v1:
time: 178 us
  Pallas kernels  177 us (99%)
    pallas_call x1, Pallas kernels, encoder_backward_call(): pl.pallas_call(functools.partial(encoder_backward_kernel, reduce), out_sh...  81.5 us
    pallas_call x1, Pallas kernels, decoder_call(): pl.pallas_call(functools.partial(decoder_kernel, reduce), out_shape=(summ...  78.1 us
    pallas_call x1, Pallas kernels, encoder_forward_call(): pl.pallas_call(encoder_forward_kernel, out_shape=(jax.ShapeDtypeStruct((2...  13.5 us
    pallas_call x1, Pallas kernels, finish_call(): pl.pallas_call(finish_kernel, out_shape=tuple((jax.ShapeDtypeStruct(shape...  3.58 us

profile of v1, /device:TPU:0, one launch (start us, length us, event | category | flops | bytes accessed | tf_op | source)
XLA Modules:
  0.0 177.7 jit_solution(8121863593359576493)
XLA Ops:
  0.7 13.5 %encoder_forward.1 = (bf16[256,768]{1,0:T(8,128)(2,1)}, f32[16,1024]{1,0:T(8,128)}, f32[2,4,32,128]{3,2,1,0:T(8,128)}, bf16[256,768]{1,0:T(8,128)(2,1)}, bf16[25...) custom-call(s32[2,4]{1,0:T(2,128)} %sizes.3, ...), custom_call_target="tpu_custom_call" | custom-call | tf_op jit(solution)/shard_map/encoder_forward/pallas_call | solution.py:475
  14.2 78.1 %decoder_block.1 = (f32[4,16,1152]{2,1,0:T(8,128)}, bf16[1,2,16,16,1536]{4,3,2,1,0:T(8,128)(2,1)}, f32[24,512]{1,0:T(8,128)}, bf16[256,768]{1,0:T(8,128)(2,1)}) custom-call(s32[2,4]{1,0:T(2,128)} %sizes.3, s32[2,256]{1,0:T(2,128)} %slots.1, f32[2,4,32,128]{3,2,1,0:T(8,128)} %get-tuple-element.62.table, bf16[256,768]{1,0:T(8,128)(2,1)} %get-tuple-element.63.sent, ...), custom_call_target="tpu_custom_call" | custom-call | tf_op jit(solution)/shard_map/decoder_block/pallas_call | solution.py:756
  92.3 81.5 %encoder_backward.1 = (f32[9,16,1536]{2,1,0:T(8,128)}, f32[2,16,768]{2,1,0:T(8,128)}, f32[16,1024]{1,0:T(8,128)}, f32[256,768]{1,0:T(8,128)}, f32[24,512]{1,0:T(8,128)}, /*index=5*/bf16[256,768]{1,0:T(8,128)(2,1)}) custom-call(bf16[256,768]{1,0:T(8,128)(2,1)} %get-tuple-element.65.encoded_grad.encoded_grad_far, f32[16,1024]{1,0:T(8,128)} %get-tuple-element.66.sums, ...), custom_call_target="tpu_custom_call" | custom-call | tf_op jit(solution)/shard_map/encoder_backward/pallas_call | solution.py:1133
  173.9 3.6 %finish.1 = (f32[1,2,256,768]{3,2,1,0:T(8,128)}, f32[1,8]{1,0:T(1,128)}, f32[2,24]{1,0:T(2,128)}, f32[2,24]{1,0:T(2,128)}, f32[2,24]{1,0:T(2,128)}, /*index=5*/f...) custom-call(f32[4,16,1152]{2,1,0:T(8,128)} %get-tuple-element.64.dec, ...), custom_call_target="tpu_custom_call" | custom-call | tf_op jit(solution)/shard_map/finish/pallas_call | solution.py:1282

commit v2 on v1

--- a/solution.py
+++ b/solution.py
@@ -21,7 +21,7 @@
 ROUTES = (("x", "y", "z1", "z2"), ("y", "x", "z1", "z2"), ("z1", "z2", "x", "y"))
 UNIT = 1536
 LAG = 2
-DECODER_PLAN = types.SimpleNamespace(widths=(3, 4, 2), chunks=4, slots=4, ring=3, span=1152)
+DECODER_PLAN = types.SimpleNamespace(widths=(2, 2, 1), chunks=7, slots=7, ring=3, span=640)
 ENCODER_PLAN = types.SimpleNamespace(widths=(3, 6, 3), chunks=9, slots=3, ring=3, span=1536)
 TAIL_PLAN = types.SimpleNamespace(widths=(2, 3, 1), chunks=2, slots=2, ring=2, span=768)
 
@@ -674,7 +674,7 @@
         for head in range(4):
             delta[head, :, rows] = row_sum(product[head * 64 : head * 64 + 64])
         if reduce:
-            engine.turn(tile - 1)
+            engine.turn(tile)
 
     for part in range(2):
         cols = slice(part * 256, part * 256 + 256)
@@ -707,7 +707,7 @@
         value_grad = dot(jnp.concatenate(probabilities, axis=1), jnp.concatenate(outers, axis=0))
         mixed_grad[rows, pair_lanes(pair, 512)] = low(value_grad)
         if reduce:
-            engine.turn(tiles - 1 + step)
+            engine.turn(tiles + step)
 
     def last(tile, entry_grad):
         rows = rows_of(tile)
@@ -721,7 +721,7 @@
         fill = validity(tile, TILE) * (1.0 - jnp.sum(spread, axis=1, keepdims=True))
         add_row(3, row_sum(fill * grad))
         if reduce:
-            engine.turn(3 * tiles - 1 + tile)
+            engine.turn(3 * tiles + tile)
         return entry_grad + dot_tn(low(spread), low(grad))
 
     entry_grad = lax.fori_loop(0, tiles, last, jnp.zeros((TILE, 512), F32))

time: 178 us -> 176 us (0.989)
  Pallas kernels: 177 us -> 175 us
    pallas_call x1, Pallas kernels: 78.1 us -> 75.1 us  [decoder_call(): pl.pallas_call(functools.partial(decoder_kernel, reduce), out_shape=(summ...]
where the time goes in v2:
time: 176 us; the launch traced here: 175 us
  Pallas kernels  175 us (99%)
    pallas_call x1, Pallas kernels, encoder_backward_call(): pl.pallas_call(functools.partial(encoder_backward_kernel, reduce), out_sh...  82.3 us
    pallas_call x1, Pallas kernels, decoder_call(): pl.pallas_call(functools.partial(decoder_kernel, reduce), out_shape=(summ...  75.1 us
    pallas_call x1, Pallas kernels, encoder_forward_call(): pl.pallas_call(encoder_forward_kernel, out_shape=(jax.ShapeDtypeStruct((2...  13.5 us
    pallas_call x1, Pallas kernels, finish_call(): pl.pallas_call(finish_kernel, out_shape=tuple((jax.ShapeDtypeStruct(shape...  3.58 us

profile of v2, /device:TPU:0, one launch (start us, length us, event | category | flops | bytes accessed | tf_op | source)
XLA Modules:
  0.0 175.4 jit_solution(4494941593586987186)
XLA Ops:
  0.7 13.5 %encoder_forward.1 = (bf16[256,768]{1,0:T(8,128)(2,1)}, f32[16,1024]{1,0:T(8,128)}, f32[2,4,32,128]{3,2,1,0:T(8,128)}, bf16[256,768]{1,0:T(8,128)(2,1)}, bf16[25...) custom-call(s32[2,4]{1,0:T(2,128)} %sizes.3, ...), custom_call_target="tpu_custom_call" | custom-call | tf_op jit(solution)/shard_map/encoder_forward/pallas_call | solution.py:475
  14.2 75.1 %decoder_block.1 = (f32[7,16,640]{2,1,0:T(8,128)}, bf16[1,2,16,16,1536]{4,3,2,1,0:T(8,128)(2,1)}, f32[24,512]{1,0:T(8,128)}, bf16[256,768]{1,0:T(8,128)(2,1)}) custom-call(s32[2,4]{1,0:T(2,128)} %sizes.3, s32[2,256]{1,0:T(2,128)} %slots.1, f32[2,4,32,128]{3,2,1,0:T(8,128)} %get-tuple-element.62.table, bf16[256,768]{1,0:T(8,128)(2,1)} %get-tuple-element.63.sent, ...), custom_call_target="tpu_custom_call" | custom-call | tf_op jit(solution)/shard_map/decoder_block/pallas_call | solution.py:756
  89.3 82.3 %encoder_backward.1 = (f32[9,16,1536]{2,1,0:T(8,128)}, f32[2,16,768]{2,1,0:T(8,128)}, f32[16,1024]{1,0:T(8,128)}, f32[256,768]{1,0:T(8,128)}, f32[24,512]{1,0:T(8,128)}, /*index=5*/bf16[256,768]{1,0:T(8,128)(2,1)}) custom-call(bf16[256,768]{1,0:T(8,128)(2,1)} %get-tuple-element.65.encoded_grad.encoded_grad_far, f32[16,1024]{1,0:T(8,128)} %get-tuple-element.66.sums, ...), custom_call_target="tpu_custom_call" | custom-call | tf_op jit(solution)/shard_map/encoder_backward/pallas_call | solution.py:1133
  171.7 3.6 %finish.1 = (f32[1,2,256,768]{3,2,1,0:T(8,128)}, f32[1,8]{1,0:T(1,128)}, f32[2,24]{1,0:T(2,128)}, f32[2,24]{1,0:T(2,128)}, f32[2,24]{1,0:T(2,128)}, /*index=5*/f...) custom-call(f32[7,16,640]{2,1,0:T(8,128)} %get-tuple-element.64.deco, ...), custom_call_target="tpu_custom_call" | custom-call | tf_op jit(solution)/shard_map/finish/pallas_call | solution.py:1282
